TPU v7x, 32 devices: a whole 2x2x4 slice. The times are simulated.
32 devices in a mesh: groups: 2 (over y), rows: 16 (over z, x, core).
Axes of the slice: x: 2, y: 2, z: 4, core: 2. Of those that a mesh axis runs over, the one named last changes fastest.
Arguments:
- embeddings: float32 [16384, 4096], P(('groups', 'rows')), parts along dimension 0
- sketch: float32 [4096, 256], replicated, may hold values from -0.09375 to 0.09375
- pair_src: int32 [8192], P(('groups', 'rows')), parts along dimension 0, may hold values from 0 to 31, as said below
- pair_tgt: int32 [8192], P(('groups', 'rows')), parts along dimension 0, may hold values from 0 to 31, as said below
- pair_count: int32 [32], P(('groups', 'rows')), parts along dimension 0, may hold values from 64 to 256, as said below
Outputs:
- best_sim: float32 [16384], P(('groups', 'rows')), parts along dimension 0
There are 2 independent parts, one for each index of `groups`. A program takes and returns all parts, laid end to end along the dimension named above; an argument that names none is the same for every part. Nothing has to cross between parts.
Inputs may be any that keep to these rules, and one draw needn't show every extreme that they name: `pair_src`: every slot of owner o names one of its own blocks, o * 2 to o * 2 + 1, and all slots of owner o whose target blocks lie on one index of rows name the same source block. `pair_tgt`: no slot of owner o names a block of o itself, and all slots of one owner that name blocks of one index of rows name the same block. `pair_count`: slots at or beyond an owner's count are not live.
All inputs are finite; a program needn't handle non-finite values.
Results may differ from a plain program's by a relative error of at most 0.00059.
Values may be sent and summed in bfloat16 or wider, within the bound.
A program may use at most 128 MiB of HBM per device.

v0:
```python
import math

import jax
import jax.numpy as jnp
from jax import lax
from jax.sharding import PartitionSpec as P

BLOCK = 256


def unit_rows(embeddings, sketch):
    sketched = jnp.dot(
        embeddings, sketch, precision=lax.Precision.HIGHEST, preferred_element_type=jnp.float32
    )
    width_total = sketched.shape[1]
    factor = lax.rsqrt(jnp.mean(sketched * sketched, axis=1, keepdims=True) + 1e-06) / math.sqrt(
        width_total
    )
    return (sketched * factor).astype(jnp.bfloat16)


def select_blocks(block_hot, blocks):
    blk_dev, block_rows, sketch_width = blocks.shape
    picked = jnp.dot(
        block_hot.astype(jnp.bfloat16),
        blocks.reshape(blk_dev, block_rows * sketch_width),
        preferred_element_type=jnp.float32,
    )
    return picked.astype(jnp.bfloat16).reshape(block_hot.shape[0], block_rows, sketch_width)


def per_device(embeddings, sketch, pair_src, pair_tgt, pair_count):
    device_count = lax.axis_size("rows")
    own_index = lax.axis_index("rows")
    rows_dev = embeddings.shape[0]
    blk_dev = rows_dev // BLOCK
    normed = unit_rows(embeddings, sketch)
    sketch_width = normed.shape[1]
    blocks = normed.reshape(blk_dev, BLOCK, sketch_width)
    slot_total = pair_src.shape[0]
    block_ids = jnp.arange(blk_dev, dtype=jnp.int32)
    device_ids = jnp.arange(device_count, dtype=jnp.int32)
    live_slots = jnp.arange(slot_total, dtype=jnp.int32) < pair_count[0]
    local_src = pair_src - own_index * blk_dev
    holder = pair_tgt // blk_dev
    within = pair_tgt % blk_dev
    holder_hot = (holder[:, None] == device_ids[None, :]) & live_slots[:, None]
    wanted = jnp.max(jnp.where(holder_hot, within[:, None], -1), axis=0)
    source_pick = jnp.max(jnp.where(holder_hot, local_src[:, None], -1), axis=0)
    row_block = jnp.arange(rows_dev, dtype=jnp.int32) // BLOCK
    group_size = 8
    group_count = device_count // group_size
    own_init = jnp.full((rows_dev,), -1.0, jnp.float32)
    asked_block = lax.all_to_all(wanted[:, None], "rows", split_axis=0, concat_axis=0, tiled=True)[
        :, 0
    ]
    ask_hot = asked_block[:, None] == block_ids[None, :]
    arrived = lax.all_to_all(
        select_blocks(ask_hot, blocks), "rows", split_axis=0, concat_axis=0, tiled=True
    )
    row_mask = source_pick[:, None] == row_block[None, :]
    grouped_targets = arrived.reshape(group_count, group_size, BLOCK, sketch_width)
    grouped_masks = row_mask.reshape(group_count, group_size, rows_dev)

    def pull_group(row_acc, group_item):
        target_group, mask_group = group_item
        scores = jnp.einsum("rk,hck->hrc", normed, target_group, preferred_element_type=jnp.float32)
        scores = jnp.where(mask_group[:, :, None], scores, -1.0)
        return (jnp.maximum(row_acc, jnp.max(scores, axis=(0, 2))), jnp.max(scores, axis=1))

    own_best, back_best = lax.scan(pull_group, own_init, (grouped_targets, grouped_masks))
    back_best = back_best.reshape(device_count, BLOCK)
    returned = lax.all_to_all(back_best, "rows", split_axis=0, concat_axis=0, tiled=True)
    returned_best = jnp.max(jnp.where(ask_hot[:, :, None], returned[:, None, :], -1.0), axis=0)
    best_sim = jnp.maximum(own_best.reshape(blk_dev, BLOCK), returned_best)
    return jnp.maximum(best_sim, -1.0).reshape(rows_dev)


def solution(mesh):
    return jax.shard_map(
        per_device,
        mesh=mesh,
        in_specs=(
            P(("groups", "rows"), None),
            P(),
            P(("groups", "rows")),
            P(("groups", "rows")),
            P(("groups", "rows")),
        ),
        out_specs=P(("groups", "rows")),
        check_vma=False,
    )
```

profile of v0, /device:TPU:0, one launch (start us, length us, event | category | flops | bytes accessed | tf_op | source)
XLA Modules:
  0.0 91.4 jit_solution(17745811426524137392)
XLA Ops:
  0.7 0.7 and_select_fusion.1
  1.4 0.1 select_reduce_fusion.3
  1.5 0.7 copy.15
  2.2 7.4 %all-to-all-start = ((s32[16,1,1]{2,1,0:T(1,128)}), s32[16,1,1]{2,1,0:T(1,128)S(1)}, u32[]{:S(2)}, u32[]{:S(2)}) async-start(s32[16,1,1]{2,1,0:T(1,128)} %copy.15), calls=%async_computation | async-start | bytes 16384 | tf_op jit(solution)/shard_map/all_to_all | solution.py:54
  9.5 10.7 %multiply_reduce_fusion = (f32[512]{0:T(512)S(1)}, f32[512,256]{0,1:T(8,128)S(1)}) fusion(f32[512,4096]{1,0:T(8,128)} %param.7, f32[4096,256]{1,0:T(8,128)} %param.8), kind=kOutput, calls=%fused_computation.12 | convolution fusion | flops 6442712576 | bytes 13109248 | tf_op jit(solution)/shard_map/dot_general | solution.py:12
  20.3 0.1 copy.16
  20.4 0.1 reshape_reshape.3
  20.5 0.0 all-to-all-done
  20.5 0.4 reduce.2
  20.9 0.8 convolution_convert_fusion
  21.7 1.8 %copy.19 = bf16[2,8,256,256]{3,2,1,0:T(8,128)(2,1)} copy(bf16[2,8,256,256]{3,1,2,0:T(8,128)(2,1)S(1)} %bitcast.36) | data formatting | bytes 4194304
  23.5 6.0 %all-to-all-start.1 = ((bf16[16,256,256]{2,1,0:T(8,128)(2,1)}), bf16[16,256,256]{2,1,0:T(8,128)(2,1)S(1)}, u32[]{:S(2)}, u32[]{:S(2)}) async-start(bf16[16,256,256]{2,1,0:T(8,128)(2,1)} %bitcast.9), calls=%async_computation.1 | async-start | bytes 4194304 | tf_op jit(solution)/shard_map/all_to_all | solution.py:58
  29.6 0.1 eq.53
  29.7 0.1 broadcast_compare_fusion
  29.7 40.9 %all-to-all-done.1 = bf16[16,256,256]{2,1,0:T(8,128)(2,1)S(1)} async-done(((bf16[16,256,256]{2,1,0:T(8,128)(2,1)}), bf16[16,256,256]{2,1,0:T(8,128)(2,1)S(1)}, u32[]{:S(2)}, u32[]{:S(2)}) %all-to-all-start.1) | async-done | bytes 2097184 | tf_op jit(solution)/shard_map/all_to_all | solution.py:58
  70.7 1.7 %while.13 = (s32[]{:T(128)}, f32[512]{0:T(512)S(1)}, f32[2,8,256]{2,1,0:T(8,128)S(1)}, pred[2,8,512]{2,1,0:T(8,128)(4,1)S(1)}, bf16[2,8,256,256]{3,2,1,0:T(8,128...) while((s32[]{:T(128)}, f32[512]{0:T(512)S(1)}, f32[2,8,256]{2,1,0:T(8,128)S(1)}, ...), condition=%wide.region_6.7_spmd.clone, body=%wide.region_3.6_spmd.clone.sunk | while | flops 540015104 | bytes 1355883 | solution.py:71
  70.7 0.8 select_reduce_fusion.6
  71.5 0.8 select_reduce_fusion.6
  72.4 0.6 all_to_all.18
  73.0 11.2 %all-to-all-start.2 = ((f32[16,1,256]{2,1,0:T(1,128)}), f32[16,1,256]{2,1,0:T(1,128)S(1)}, u32[]{:S(2)}, u32[]{:S(2)}) async-start(f32[16,1,256]{2,1,0:T(1,128)} %all_to_all.18), calls=%async_computation.2 | async-start | bytes 32768 | tf_op jit(solution)/shard_map/all_to_all | solution.py:73
  84.3 6.5 %all-to-all-done.2 = f32[16,1,256]{2,1,0:T(1,128)S(1)} async-done(((f32[16,1,256]{2,1,0:T(1,128)}), f32[16,1,256]{2,1,0:T(1,128)S(1)}, u32[]{:S(2)}, u32[]{:S(2)}) %all-to-all-start.2) | async-done | bytes 16416 | tf_op jit(solution)/shard_map/all_to_all | solution.py:73
  90.7 0.1 select_reduce_fusion.2
  90.8 0.6 maximum_maximum_fusion
  (15 shorter events, 0.1 us)
Async XLA Ops:
  2.2 18.3 %all-to-all-start = ((s32[16,1,1]{2,1,0:T(1,128)}), s32[16,1,1]{2,1,0:T(1,128)S(1)}, u32[]{:S(2)}, u32[]{:S(2)}) async-start(s32[16,1,1]{2,1,0:T(1,128)} %copy.15), calls=%async_computation | async-start | bytes 16384 | tf_op jit(solution)/shard_map/all_to_all | solution.py:54
  23.5 47.1 %all-to-all-start.1 = ((bf16[16,256,256]{2,1,0:T(8,128)(2,1)}), bf16[16,256,256]{2,1,0:T(8,128)(2,1)S(1)}, u32[]{:S(2)}, u32[]{:S(2)}) async-start(bf16[16,256,256]{2,1,0:T(8,128)(2,1)} %bitcast.9), calls=%async_computation.1 | async-start | bytes 4194304 | tf_op jit(solution)/shard_map/all_to_all | solution.py:58
  73.0 17.7 %all-to-all-start.2 = ((f32[16,1,256]{2,1,0:T(1,128)}), f32[16,1,256]{2,1,0:T(1,128)S(1)}, u32[]{:S(2)}, u32[]{:S(2)}) async-start(f32[16,1,256]{2,1,0:T(1,128)} %all_to_all.18), calls=%async_computation.2 | async-start | bytes 32768 | tf_op jit(solution)/shard_map/all_to_all | solution.py:73
where the time goes:
time: 91.7 us; the launch traced here: 91.4 us
  waiting for transfers between devices  47.4 us (52%)
  starting transfers between devices  24.6 us (27%)
  matrix products  13.1 us (14%)
  local copies, waits for them, and re-layouts  3.43 us (4%)
  other arithmetic  2.06 us (2%)
    all_to_all x1, waiting for transfers between devices, per_device(): lax.all_to_all(select_blocks(ask_hot, blocks), 'rows', split_axis=0, conc...  40.9 us
    all_to_all x1, starting transfers between devices, per_device(): lax.all_to_all(back_best, 'rows', split_axis=0, concat_axis=0, tiled=True)  11.2 us
    dot_general x1, matrix products, unit_rows(): jnp.dot(embeddings, sketch, precision=lax.Precision.HIGHEST, preferred_el...  10.7 us
    all_to_all x1, starting transfers between devices, per_device(): lax.all_to_all(wanted[:, None], 'rows', split_axis=0, concat_axis=0, tile...  7.36 us
    all_to_all x1, waiting for transfers between devices, per_device(): lax.all_to_all(back_best, 'rows', split_axis=0, concat_axis=0, tiled=True)  6.48 us
    all_to_all x1, starting transfers between devices, per_device(): lax.all_to_all(select_blocks(ask_hot, blocks), 'rows', split_axis=0, conc...  6 us
  transfers between devices with their start and end apart: 3, of which 2 were waited for; matrix products, arithmetic and copies ran while one was open for 12% of the time, Pallas kernels for 0%

commit v1 on v0

v1 whole, which is shorter than its diff:
```python
import functools
import math

import jax
import jax.numpy as jnp
from jax import lax
from jax.experimental import pallas as pl
from jax.experimental.pallas import tpu as pltpu
from jax.sharding import PartitionSpec as P

BLOCK = 256
K_TILE = 1024
NEG = -1.0


def chip_of(place, half):
    side = lax.div(place, half)
    return (place + side * (2 * half - 1 - 2 * place)) * 2 + side


def place_of(chip, half):
    side = lax.rem(chip, 2)
    level = lax.div(chip, 2)
    return level + side * (2 * half - 1 - 2 * level)


def kernel(
    device_count,
    chunk_rows,
    count_ref,
    src_ref,
    tgt_ref,
    emb_ref,
    sketch_ref,
    out_ref,
    emb,
    sketch,
    high,
    low,
    chain,
    mirror,
    best,
    emb_sem,
    sketch_sem,
    chain_send,
    chain_recv,
    mirror_send,
    mirror_recv,
):
    rows_dev, embed = emb.shape
    width = sketch.shape[1]
    chunk_count = rows_dev // chunk_rows
    chip_count = device_count // 2
    half = chip_count // 2
    blk_dev = rows_dev // BLOCK
    k_tile = min(K_TILE, embed)
    k_count = embed // k_tile

    emb_copies = [
        pltpu.make_async_copy(
            emb_ref.at[pl.ds(c * chunk_rows, chunk_rows)],
            emb.at[pl.ds(c * chunk_rows, chunk_rows)],
            emb_sem.at[c],
        )
        for c in range(chunk_count)
    ]
    sketch_copies = [
        pltpu.make_async_copy(
            sketch_ref.at[pl.ds(k * k_tile, k_tile)],
            sketch.at[pl.ds(k * k_tile, k_tile)],
            sketch_sem.at[k],
        )
        for k in range(k_count)
    ]
    emb_copies[0].start()
    for copy in sketch_copies:
        copy.start()
    for copy in emb_copies[1:]:
        copy.start()

    me = lax.axis_index("rows")
    core = lax.rem(me, 2)
    place = place_of(lax.div(me, 2), half)
    turn = 1 - 2 * core
    after = chip_of(lax.rem(place + turn + chip_count, chip_count), half) * 2 + core
    before = chip_of(lax.rem(place - turn + chip_count, chip_count), half) * 2 + core
    sibling = me + turn

    barrier = pltpu.get_barrier_semaphore()
    for other in (before, sibling):
        pl.semaphore_signal(
            barrier, inc=1, device_id={"rows": other}, device_id_type=pl.DeviceIdType.MESH
        )

    slots = src_ref.shape[1]
    live = lax.broadcasted_iota(jnp.int32, (1, slots), 1) < count_ref[0]
    local_src = src_ref[...] - me * blk_dev
    holder_first = lax.broadcasted_iota(jnp.int32, (device_count, slots), 0) * blk_dev
    codes = jnp.full((device_count, slots), -1, jnp.int32)
    for t in range(blk_dev):
        hit = (tgt_ref[...] == holder_first + t) & live
        codes = jnp.maximum(codes, jnp.where(hit, local_src * blk_dev + t, -1))
    codes = jnp.max(codes.astype(jnp.float32), axis=1, keepdims=True)
    chain[0, pl.ds(0, device_count), :] = jnp.broadcast_to(codes, (device_count, width)).astype(
        jnp.bfloat16
    )
    best[...] = jnp.full(best.shape, NEG, jnp.float32)

    def span(c):
        if c == 0:
            return pl.ds(0, device_count + chunk_rows)
        return pl.ds(device_count + c * chunk_rows, chunk_rows)

    def onward(hop, c):
        return pltpu.make_async_remote_copy(
            src_ref=chain.at[hop, span(c)],
            dst_ref=chain.at[hop + 1, span(c)],
            send_sem=chain_send.at[hop, c],
            recv_sem=chain_recv.at[hop, c],
            device_id={"rows": after},
            device_id_type=pl.DeviceIdType.MESH,
        )

    def across(hop, c):
        return pltpu.make_async_remote_copy(
            src_ref=chain.at[hop, span(c)],
            dst_ref=mirror.at[hop, span(c)],
            send_sem=mirror_send.at[hop, c],
            recv_sem=mirror_recv.at[hop, c],
            device_id={"rows": sibling},
            device_id_type=pl.DeviceIdType.MESH,
        )

    for c in range(chunk_count):
        emb_copies[c].wait()
        total = jnp.zeros((chunk_rows, width), jnp.float32)
        for k in range(k_count):
            depth = pl.ds(k * k_tile, k_tile)
            if c == 0:
                sketch_copies[k].wait()
                value = sketch[depth, :]
                top = value.astype(jnp.bfloat16)
                high[depth, :] = top
                low[depth, :] = (value - top.astype(jnp.float32)).astype(jnp.bfloat16)
            value = emb[pl.ds(c * chunk_rows, chunk_rows), depth]
            top = value.astype(jnp.bfloat16)
            rest = (value - top.astype(jnp.float32)).astype(jnp.bfloat16)
            total += jnp.dot(top, low[depth, :], preferred_element_type=jnp.float32)
            total += jnp.dot(rest, high[depth, :], preferred_element_type=jnp.float32)
            total += jnp.dot(top, high[depth, :], preferred_element_type=jnp.float32)
        mean = jnp.sum(total * total, axis=1, keepdims=True) * (1.0 / width)
        factor = lax.rsqrt(mean + 1e-06) * (1.0 / math.sqrt(width))
        chain[0, pl.ds(device_count + c * chunk_rows, chunk_rows), :] = (total * factor).astype(
            jnp.bfloat16
        )
        if c == 0:
            pl.semaphore_wait(barrier, 2)
        onward(0, c).start()
        across(0, c).start()

    def row_of(table, index):
        ids = lax.broadcasted_iota(jnp.int32, (device_count, width), 0)
        picked = jnp.where(ids == index, table.astype(jnp.float32), NEG)
        return jnp.max(picked, axis=0, keepdims=True)

    lane_block = lax.broadcasted_iota(jnp.int32, (1, rows_dev), 1)
    own_block = jnp.zeros((1, rows_dev), jnp.float32)
    for b in range(1, blk_dev):
        own_block += jnp.where(lane_block >= b * BLOCK, 1.0, 0.0)

    def score(held, hop, c, device):
        mine = row_of(chain[0, pl.ds(0, device_count), :], device)
        theirs = row_of(held[hop, pl.ds(0, device_count), :], me)
        repeat = rows_dev // width
        mine = jnp.concatenate([mine] * repeat, axis=1)
        theirs = jnp.concatenate([theirs] * repeat, axis=1)
        part = (c * chunk_rows) // BLOCK
        remote = held[hop, pl.ds(device_count + c * chunk_rows, chunk_rows), :]
        own = chain[0, pl.ds(device_count, rows_dev), :]
        tile = lax.dot_general(
            remote, own, (((1,), (1,)), ((), ())), preferred_element_type=jnp.float32
        )
        tile = jnp.max(tile.reshape(chunk_rows // 8, 8, rows_dev), axis=0)
        linked = (mine == own_block * blk_dev + part) | (theirs == own_block + part * blk_dev)
        best[...] = jnp.maximum(best[...], jnp.where(linked, tile, NEG))

    def chain_device(hop):
        return chip_of(lax.rem(place - turn * hop + chip_count, chip_count), half) * 2 + core

    def mirror_device(hop):
        return chip_of(lax.rem(place + turn * hop + chip_count, chip_count), half) * 2 + 1 - core

    def mirror_step(hop, c):
        across(hop, c).wait_recv()
        score(mirror, hop, c, mirror_device(hop))

    for c in range(chunk_count - 1):
        mirror_step(0, c)

    def hop_step(hop, last):
        for c in range(chunk_count):
            onward(hop - 1, c).wait_recv()
            if not last:
                onward(hop, c).start()
            across(hop, c).start()
            score(chain, hop, c, chain_device(hop))
            if c == 0:
                mirror_step(hop - 1, chunk_count - 1)
            else:
                mirror_step(hop, c - 1)

    def body(hop, carry):
        hop_step(hop, False)
        return carry

    lax.fori_loop(1, chip_count - 1, body, 0)
    hop_step(chip_count - 1, True)
    mirror_step(chip_count - 1, chunk_count - 1)
    out_ref[...] = jnp.max(best[...], axis=0, keepdims=True)

    def drain(hop, carry):
        for c in range(chunk_count):
            onward(hop, c).wait_send()
            across(hop, c).wait_send()
        return carry

    lax.fori_loop(0, chip_count - 1, drain, 0)
    for c in range(chunk_count):
        across(chip_count - 1, c).wait_send()


def per_device(embeddings, sketch, pair_src, pair_tgt, pair_count):
    device_count = lax.axis_size("rows")
    rows_dev, embed = embeddings.shape
    width = sketch.shape[1]
    chip_count = device_count // 2
    chunk_rows = 128 if chip_count <= 8 else 256
    chunks = rows_dev // chunk_rows
    item = (chip_count, device_count + rows_dev, width)
    slots = pair_src.shape[0]
    vmem = pl.BlockSpec(memory_space=pltpu.VMEM)
    best = pl.pallas_call(
        functools.partial(kernel, device_count, chunk_rows),
        out_shape=jax.ShapeDtypeStruct((1, rows_dev), jnp.float32),
        in_specs=[
            pl.BlockSpec(memory_space=pltpu.SMEM),
            vmem,
            vmem,
            pl.BlockSpec(memory_space=pl.ANY),
            pl.BlockSpec(memory_space=pl.ANY),
        ],
        out_specs=vmem,
        scratch_shapes=[
            pltpu.VMEM((rows_dev, embed), jnp.float32),
            pltpu.VMEM((embed, width), jnp.float32),
            pltpu.VMEM((embed, width), jnp.bfloat16),
            pltpu.VMEM((embed, width), jnp.bfloat16),
            pltpu.VMEM(item, jnp.bfloat16),
            pltpu.VMEM(item, jnp.bfloat16),
            pltpu.VMEM((8, rows_dev), jnp.float32),
            pltpu.SemaphoreType.DMA((chunks,)),
            pltpu.SemaphoreType.DMA((embed // min(K_TILE, embed),)),
            pltpu.SemaphoreType.DMA((chip_count, chunks)),
            pltpu.SemaphoreType.DMA((chip_count, chunks)),
            pltpu.SemaphoreType.DMA((chip_count, chunks)),
            pltpu.SemaphoreType.DMA((chip_count, chunks)),
        ],
        compiler_params=pltpu.CompilerParams(
            collective_id=0, has_side_effects=True, vmem_limit_bytes=60 * 1024 * 1024
        ),
    )(pair_count, pair_src.reshape(1, slots), pair_tgt.reshape(1, slots), embeddings, sketch)
    return best.reshape(rows_dev)


def solution(mesh):
    return jax.shard_map(
        per_device,
        mesh=mesh,
        in_specs=(
            P(("groups", "rows"), None),
            P(),
            P(("groups", "rows")),
            P(("groups", "rows")),
            P(("groups", "rows")),
        ),
        out_specs=P(("groups", "rows")),
        check_vma=False,
    )
```

time: 91.7 us -> 41.6 us (0.45)
  waiting for transfers between devices: 47.4 us -> 0 us
  Pallas kernels: 0 us -> 39.5 us
  starting transfers between devices: 24.6 us -> 0 us
  matrix products: 13.1 us -> 0 us
  local copies, waits for them, and re-layouts: 3.43 us -> 1.26 us
  other arithmetic: 2.06 us -> 0 us
    all_to_all x3 -> x0, waiting for transfers between devices: 47.4 us -> none  [the longest x1 40.9 us: per_device(): lax.all_to_all(select_blocks(ask_hot, blocks), 'rows', split_axis=0, conc...]
    pallas_call x0 -> x1, Pallas kernels: none -> 39.5 us  [per_device(): pl.pallas_call(functools.partial(kernel, device_count, chunk_rows), out_s...]
    all_to_all x3 -> x0, starting transfers between devices: 24.6 us -> none  [the longest x1 11.2 us: per_device(): lax.all_to_all(back_best, 'rows', split_axis=0, concat_axis=0, tiled=True)]
    dot_general x4 -> x0, matrix products: 13.1 us -> none  [the longest x1 10.7 us: unit_rows(): jnp.dot(embeddings, sketch, precision=lax.Precision.HIGHEST, preferred_el...]
    all_to_all x2 -> x0, local copies, waits for them, and re-layouts: 1.29 us -> none  [the longest x1 0.68 us: per_device(): lax.all_to_all(wanted[:, None], 'rows', split_axis=0, concat_axis=0, tile...]
  transfers between devices with their start and end apart: 3 -> 0, of which waited for: 2 -> 0; matrix products, arithmetic and copies ran while one was open for 12% -> 0% of each run, Pallas kernels for 0% -> 0%
where the time goes in v1:
time: 41.6 us; the launch traced here: 41.4 us
  Pallas kernels  39.5 us (95%)
  local copies, waits for them, and re-layouts  1.26 us (3%)
  between operations  0.66 us (2%)
    pallas_call x1, Pallas kernels, per_device(): pl.pallas_call(functools.partial(kernel, device_count, chunk_rows), out_s...  39.5 us
    unnamed x1, local copies, waits for them, and re-layouts  1.26 us

profile of v1, /device:TPU:0, one launch (start us, length us, event | category | flops | bytes accessed | tf_op | source)
XLA Modules:
  0.0 41.4 jit_solution(9667040005863504222)
XLA Ops:
  0.7 39.5 %shard_map.55 = f32[1,512]{1,0:T(1,128)} custom-call(s32[1]{0:T(128)S(6)} %copy.7.count_ref, s32[1,256]{1,0:T(1,128)} %bitcast.4, s32[1,256]{1,0:T(1,128)} %bitcast.5, f32[512,4096]{1,0:T(8,128)} %emb_ref.1, f32[4096,256]{1,0:T(8,128)} %sketch_ref.1), custom_call_target="tpu_custom_call" | custom-call | tf_op jit(solution)/shard_map/pallas_call | solution.py:242
  40.2 1.3 %copy.8 = f32[512]{0:T(512)} copy(f32[512]{0:T(512)} %bitcast.3) | data formatting | bytes 4096

commit v2 on v1

--- a/solution.py
+++ b/solution.py
@@ -72,10 +72,9 @@
         )
         for k in range(k_count)
     ]
-    emb_copies[0].start()
     for copy in sketch_copies:
         copy.start()
-    for copy in emb_copies[1:]:
+    for copy in emb_copies:
         copy.start()
 
     me = lax.axis_index("rows")
@@ -216,7 +215,7 @@
     lax.fori_loop(1, chip_count - 1, body, 0)
     hop_step(chip_count - 1, True)
     mirror_step(chip_count - 1, chunk_count - 1)
-    out_ref[...] = jnp.max(best[...], axis=0, keepdims=True)
+    out_ref[...] = best[...]
 
     def drain(hop, carry):
         for c in range(chunk_count):
@@ -241,7 +240,7 @@
     vmem = pl.BlockSpec(memory_space=pltpu.VMEM)
     best = pl.pallas_call(
         functools.partial(kernel, device_count, chunk_rows),
-        out_shape=jax.ShapeDtypeStruct((1, rows_dev), jnp.float32),
+        out_shape=jax.ShapeDtypeStruct((8, rows_dev), jnp.float32),
         in_specs=[
             pl.BlockSpec(memory_space=pltpu.SMEM),
             vmem,
@@ -269,7 +268,7 @@
             collective_id=0, has_side_effects=True, vmem_limit_bytes=60 * 1024 * 1024
         ),
     )(pair_count, pair_src.reshape(1, slots), pair_tgt.reshape(1, slots), embeddings, sketch)
-    return best.reshape(rows_dev)
+    return jnp.max(best, axis=0)
 
 
 def solution(mesh):

time: 41.6 us -> 41.8 us (level)
  other arithmetic: 0 us -> 1.31 us
  local copies, waits for them, and re-layouts: 1.26 us -> 0 us
    reduce_max x0 -> x1, other arithmetic: none -> 1.31 us  [per_device(): return jnp.max(best, axis=0)]
    unnamed x1 -> x0, local copies, waits for them, and re-layouts: 1.26 us -> none
where the time goes in v2:
time: 41.8 us; the launch traced here: 41.5 us
  Pallas kernels  39.5 us (94%)
  other arithmetic  1.31 us (3%)
  between operations  0.66 us (2%)
    pallas_call x1, Pallas kernels, per_device(): pl.pallas_call(functools.partial(kernel, device_count, chunk_rows), out_s...  39.5 us
    reduce_max x1, other arithmetic, per_device(): return jnp.max(best, axis=0)  1.31 us

profile of v2, /device:TPU:0, one launch (start us, length us, event | category | flops | bytes accessed | tf_op | source)
XLA Modules:
  0.0 41.5 jit_solution(209830505326876576)
XLA Ops:
  0.7 39.5 %shard_map.55 = f32[8,512]{1,0:T(8,128)} custom-call(s32[1]{0:T(128)S(6)} %copy.6.count_ref, s32[1,256]{1,0:T(1,128)} %bitcast.2, s32[1,256]{1,0:T(1,128)} %bitcast.3, f32[512,4096]{1,0:T(8,128)} %emb_ref.1, f32[4096,256]{1,0:T(8,128)} %sketch_ref.1), custom_call_target="tpu_custom_call" | custom-call | tf_op jit(solution)/shard_map/pallas_call | solution.py:241
  40.2 1.3 %reduce_max.9 = f32[512]{0:T(512)} reduce(f32[8,512]{1,0:T(8,128)} %shard_map.55, f32[]{:T(128)} %constant.0.clone.1), dimensions={0}, to_apply=%region_0.0 | reduce | flops 3584 | bytes 18436 | tf_op jit(solution)/shard_map/reduce_max | solution.py:271
